TPU v7x, 32 devices: a whole 2x2x4 slice. The times are simulated.
32 devices in a mesh: groups: 2 (over x), gx: 8 (over z, y), gy: 2 (over core).
Axes of the slice: x: 2, y: 2, z: 4, core: 2. Of those that a mesh axis runs over, the one named last changes fastest.
Arguments:
- plume_state: bfloat16 [4, 20, 32, 256, 128], P('groups', None, 'gx', 'gy'), parts along dimension 0, may hold values from -6 to 6
- spectral_weight: bfloat16 [2, 128, 24, 800], P('gy', 'gx'), may hold values from -8 to 8
- pointwise_weight: bfloat16 [20, 20], replicated, may hold values from -1.25 to 1.25
- channel_bias: float32 [20], replicated, may hold values from -3 to 3
Outputs:
- next_state: bfloat16 [4, 20, 32, 256, 128], P('groups', None, 'gx', 'gy'), parts along dimension 0
There are 2 independent parts, one for each index of `groups`. A program takes and returns all parts, laid end to end along the dimension named above; an argument that names none is the same for every part. Nothing has to cross between parts.
All inputs are finite; a program needn't handle non-finite values.
Results may differ from a plain program's by a relative error of at most 0.014.
Values may be sent and summed in bfloat16 or wider, within the bound.
A program may use at most 128 MiB of HBM per device.

v0:
```python
import math

import jax
import jax.numpy as jnp
from jax import lax
from jax.sharding import PartitionSpec as P

MX = 24
MY = 16
MZ = 16


def retained(kept, length):
    indices = jnp.arange(kept, dtype=jnp.int32)
    return jnp.where(indices < kept // 2, indices, length - kept + indices)


def phases(freq_ids, positions, length):
    product = freq_ids[:, None] * positions[None, :] % length
    return 2.0 * math.pi / length * product.astype(jnp.float32)


def forward_table(freq_ids, positions, length):
    angles = phases(freq_ids, positions, length).T
    cosine = jnp.cos(angles)
    sine_part = jnp.sin(angles)
    stacked = jnp.stack([jnp.stack([cosine, -sine_part], 1), jnp.stack([sine_part, cosine], 1)], 1)
    return stacked.astype(jnp.bfloat16)


def inverse_table(freq_ids, positions, length):
    angles = phases(freq_ids, positions, length)
    cosine = jnp.cos(angles)
    sine_part = jnp.sin(angles)
    stacked = jnp.stack([jnp.stack([cosine, sine_part], 1), jnp.stack([-sine_part, cosine], 1)], 0)
    return stacked.astype(jnp.bfloat16)


def depth_tables(depth):
    angles = phases(jnp.arange(MZ, dtype=jnp.int32), jnp.arange(depth, dtype=jnp.int32), depth)
    cosine = jnp.cos(angles)
    sine_part = jnp.sin(angles)
    forward = jnp.concatenate([cosine.T, -sine_part.T], 1).astype(jnp.bfloat16)
    doubling = jnp.where(jnp.arange(MZ) == 0, 1.0, 2.0).astype(jnp.float32)[:, None]
    inverse = jnp.stack([doubling * cosine, -doubling * sine_part], 0).astype(jnp.bfloat16)
    return (forward, inverse)


def body(plume_state, spectral_weight, pointwise_weight, channel_bias):
    snapshots, channels, rows_x, rows_y, depth = plume_state.shape
    length_x = rows_x * lax.axis_size("gx")
    length_y = rows_y * lax.axis_size("gy")
    own_x = lax.axis_index("gx") * rows_x + jnp.arange(rows_x, dtype=jnp.int32)
    own_y = lax.axis_index("gy") * rows_y + jnp.arange(rows_y, dtype=jnp.int32)
    z_forward, z_inverse = depth_tables(depth)
    pointwise_part = jnp.einsum(
        "tcxyz,cd->tdxyz", plume_state, pointwise_weight, preferred_element_type=jnp.float32
    )
    pointwise_part = pointwise_part + channel_bias[None, :, None, None, None]
    depth_modes = jnp.einsum(
        "tcxyz,zk->tcxky", plume_state, z_forward, preferred_element_type=jnp.float32
    )
    depth_modes = depth_modes.astype(jnp.bfloat16).reshape(
        snapshots, channels, rows_x, 2, MZ, rows_y
    )
    y_forward = forward_table(retained(MY, length_y), own_y, length_y)
    row_terms = jnp.einsum(
        "tcxpky,ypqm->tcxqkm", depth_modes, y_forward, preferred_element_type=jnp.float32
    )
    row_terms = row_terms.reshape(snapshots, channels, rows_x, 2, MZ * MY)
    row_modes = lax.psum_scatter(
        row_terms.astype(jnp.bfloat16), "gy", scatter_dimension=4, tiled=True
    )
    pair_rows = spectral_weight.shape[1]
    x_local = forward_table(retained(MX, length_x), own_x, length_x)
    term = jnp.einsum("tcxpf,xpqk->ftcqk", row_modes, x_local, preferred_element_type=jnp.float32)
    summed = lax.psum_scatter(
        term.reshape(pair_rows * lax.axis_size("gx"), -1), "gx", scatter_dimension=0, tiled=True
    )
    pair_modes = summed.astype(jnp.bfloat16).reshape(pair_rows, snapshots, channels, 2, MX)
    spectral = spectral_weight.reshape(pair_rows, MX, 2, channels, channels)
    weight_real = spectral[:, :, 0]
    weight_imag = spectral[:, :, 1]
    mode_real = pair_modes[:, :, :, 0]
    mode_imag = pair_modes[:, :, :, 1]
    mixed_real = jnp.einsum(
        "ftck,fkcd->ftdk", mode_real, weight_real, preferred_element_type=jnp.float32
    ) - jnp.einsum("ftck,fkcd->ftdk", mode_imag, weight_imag, preferred_element_type=jnp.float32)
    mixed_imag = jnp.einsum(
        "ftck,fkcd->ftdk", mode_real, weight_imag, preferred_element_type=jnp.float32
    ) + jnp.einsum("ftck,fkcd->ftdk", mode_imag, weight_real, preferred_element_type=jnp.float32)
    mixed_modes = jnp.stack([mixed_real, mixed_imag], 3).astype(jnp.bfloat16)
    x_back = inverse_table(retained(MX, length_x), own_x, length_x)
    cells_x = jnp.einsum(
        "ftdqk,qkpx->tdxpf",
        lax.all_gather(mixed_modes, "gx", axis=0, tiled=True),
        x_back,
        preferred_element_type=jnp.float32,
    ).astype(jnp.bfloat16)
    both_halves = lax.all_gather(cells_x, "gy", axis=4, tiled=True)
    both_halves = both_halves.reshape(snapshots, channels, rows_x, 2, MZ, MY)
    y_back = inverse_table(retained(MY, length_y), own_y, length_y)
    cells_y = jnp.einsum(
        "tdxqkm,qmpy->tdxpky", both_halves, y_back, preferred_element_type=jnp.float32
    ).astype(jnp.bfloat16)
    inverse_size = 1.0 / (length_x * length_y * depth)
    spectral_part = (
        jnp.einsum("tdxpky,pkz->tdxyz", cells_y, z_inverse, preferred_element_type=jnp.float32)
        * inverse_size
    )
    return jax.nn.gelu(spectral_part + pointwise_part, approximate=False).astype(jnp.bfloat16)


def solution(mesh):
    placed = (P("groups", None, "gx", "gy", None), P("gy", "gx", None, None), P(), P())
    return jax.shard_map(
        body,
        mesh=mesh,
        in_specs=placed,
        out_specs=P("groups", None, "gx", "gy", None),
        check_vma=False,
    )
```

profile of v0, /device:TPU:0, one launch (start us, length us, event | category | flops | bytes accessed | tf_op | source)
XLA Modules:
  0.0 263.8 jit_solution(9334112766479745477)
XLA Ops:
  6.6 0.1 negate_convert_fusion.1
  6.8 4.4 %convolution_convert_fusion = bf16[32,2,20,4,128]{4,0,3,2,1:T(8,128)(2,1)S(1)} fusion(bf16[2,20,4,128,128]{4,3,2,1,0:T(8,128)(2,1)} %param.4, bf16[128,16]{0,1:T(8,128)(2,1)S(1)} %get-tuple-element.27, bf16[128,16]{0,1:T(8,128)(2,1)S(1)} %get-tuple-element.28), kind=kOutput, calls=%fused_computation.34 | convolution fusion | flops 168443904 | bytes 6561792 | tf_op jit(solution)/shard_map/tcxyz,zk->tcxky/dot_general | solution.py:60
  11.2 1.7 bitcast_convert_fusion.1
  12.9 10.4 %copy.78 = bf16[2,20,4,2,256]{2,3,1,0,4:T(2,128)(2,1)} copy(bf16[2,20,4,2,256]{1,4,2,0,3:T(8,128)(2,1)S(1)} %bitcast.176) | data formatting | bytes 327680
  23.3 13.9 %reshape.833 = bf16[256,320]{1,0:T(8,128)(2,1)} reshape(bf16[256,2,20,2,4]{4,3,2,1,0:T(2,128)(2,1)} %bitcast.173) | data formatting | bytes 327680
  37.3 0.3 reduce-scatter.9.cloned.1.call-start
  37.7 9.9 %reduce-scatter.7.cloned.1.call-done = bf16[128,320]{1,0:T(8,128)(2,1)} async-done(((bf16[256,320]{1,0:T(8,128)(2,1)}), bf16[128,320]{1,0:T(8,128)(2,1)}) %reduce-scatter.7.cloned.1.call-update) | async-done | bytes 81936
  47.7 8.1 %reshape.834 = bf16[128,2,20,2,4]{4,3,2,1,0:T(2,128)(2,1)S(1)} reshape(bf16[128,320]{1,0:T(8,128)(2,1)} %reduce-scatter.7.cloned.1.call-done) | data formatting | bytes 163840
  55.8 2.0 copy.79
  57.8 0.3 convolution_bitcast_fusion
  58.2 1.4 copy.80
  59.6 6.1 %reshape.814 = bf16[16,24,2,20,20]{4,3,2,1,0:T(8,128)(2,1)} reshape(bf16[1,16,24,800]{3,2,1,0:T(8,128)(2,1)S(1)} %copy-done.1) | data formatting | bytes 1228800 | tf_op jit(solution)/shard_map/reshape | solution.py:81
  65.8 0.1 fusion.80
  66.1 11.3 %fusion.10 = f32[20,2,4,128,128]{4,0,3,2,1:T(8,128)} fusion(bf16[2,20,4,128,128]{4,3,2,1,0:T(8,128)(2,1)} %param.4, bf16[20,20]{1,0:T(8,128)(2,1)S(1)} %copy-done), kind=kOutput, calls=%fused_computation.22 | convolution fusion | flops 104857600 | bytes 15729440 | tf_op jit(solution)/shard_map/tcxyz,cd->tdxyz/dot_general | solution.py:56
  77.4 46.9 %reduce-scatter.9.cloned.1.call-done = f32[16,1920]{1,0:T(8,128)} async-done(((f32[128,1920]{1,0:T(8,128)}), f32[16,1920]{1,0:T(8,128)}) %reduce-scatter.9.cloned.1.call-update) | async-done | bytes 122896 | tf_op jit(solution)/shard_map/reduce_scatter | solution.py:77
  124.2 0.9 convert_element_type.146
  125.1 0.4 reshape.813
  125.6 0.5 fusion.98
  126.0 0.5 copy.83
  126.5 14.0 %copy.85 = bf16[16,2,20,1,24]{2,1,4,0,3:T(2,128)(2,1)S(1)} copy(bf16[16,2,20,1,24]{4,3,2,1,0:T(2,128)(2,1)S(1)} %get-tuple-element.6) | data formatting | bytes 61440
  140.5 2.5 fusion.14
  143.0 2.5 fusion.15
  145.6 2.6 fusion.27
  148.2 2.6 fusion.26
  150.8 0.7 pad_maximum_fusion
  151.4 61.6 %all_gather.6 = bf16[128,2,20,2,24]{2,1,4,0,3:T(2,128)(2,1)S(1)} all-gather(bf16[16,2,20,2,24]{2,1,4,0,3:T(2,128)(2,1)S(1)} %pad_maximum_fusion), channel_id=1, replica_groups=mesh['groups'=2,'gx'=8,'gy'=2] {'gx'}, dimensions={0}, use_global_device_ids=true | all-gather | bytes 552960 | tf_op jit(solution)/shard_map/all_gather | solution.py:96
  213.0 7.4 %copy.59 = bf16[128,2,20,2,24]{4,0,3,2,1:T(8,128)(2,1)} copy(bf16[128,2,20,2,24]{2,1,4,0,3:T(2,128)(2,1)S(1)} %all_gather.6) | data formatting | bytes 983040 | tf_op jit(solution)/shard_map/all_gather | solution.py:96
  220.5 2.5 fusion.34
  223.0 1.9 all_gather.7
  224.9 0.2 copy.60
  225.1 0.9 reshape.827
  226.0 30.8 %fusion.2 = bf16[2,20,4,128,128]{4,3,2,1,0:T(8,128)(2,1)} fusion(f32[20,2,4,128,128]{4,0,3,2,1:T(8,128)} %fusion.10, f32[20]{0:T(128)S(1)} %copy-done.2, bf16[2,20,4,2,16,16,1]{5,4,3,2,1,0,6:T(8,128)(2,1)S(1)} %reshape.827, bf16[1,16,2,128]{3,1,0,2:T(8,128)(2,1)S(1)} %get-tuple-element.8, bf16[1,16,2,128]{3,1,0,2:T(8,128)(2,1)S(1)} %get-tuple-element.7, ...), kind=kOutput, calls=%fused_computation.3 | convolution fusion | flops 388665344 | bytes 15917136 | tf_op jit(solution)/shard_map/tdxpky,pkz->tdxyz/dot_general | solution.py:108
  (24 shorter events, 0.6 us)
Async XLA Ops:
  6.5 59.5 %copy-start = (bf16[20,20]{1,0:T(8,128)(2,1)S(1)}, bf16[20,20]{1,0:T(8,128)(2,1)}, u32[]{:S(2)}) copy-start(bf16[20,20]{1,0:T(8,128)(2,1)} %param.6) | copy-start | bytes 2404
  6.5 41.2 %reduce-scatter.7.cloned.1.call-start = ((), (), s32[]{:S(2)}) async-start(), calls=%async_computation.2 | async-start | bytes 294912
  12.9 46.8 %copy-start.1 = (bf16[1,16,24,800]{3,2,1,0:T(8,128)(2,1)S(1)}, bf16[1,16,24,800]{3,2,1,0:T(8,128)(2,1)}, u32[]{:S(2)}) copy-start(bf16[1,16,24,800]{3,2,1,0:T(8,128)(2,1)} %param.5) | copy-start | bytes 1843204
  37.3 86.9 %reduce-scatter.9.cloned.1.call-start = ((), (), s32[]{:S(2)}) async-start(), calls=%async_computation.3 | async-start | bytes 1105920 | tf_op jit(solution)/shard_map/reduce_scatter | solution.py:77
  145.6 80.4 %copy-start.2 = (f32[20]{0:T(128)S(1)}, f32[20]{0:T(128)}, u32[]{:S(2)}) copy-start(f32[20]{0:T(128)} %param.7) | copy-start | bytes 244
Sparse Core Ops, SparseCore 0:
  37.4 10.2 reduce-scatter.6
  59.7 64.4 reduce-scatter.8
where the time goes:
time: 263 us; the launch traced here: 264 us
  local copies, waits for them, and re-layouts  65.8 us (25%)
  blocking collectives  63.5 us (24%)
  matrix products  61.3 us (23%)
  waiting for transfers between devices  56.8 us (22%)
  between operations  13.8 us (5%)
    all_gather x1, blocking collectives, body(): lax.all_gather(mixed_modes, 'gx', axis=0, tiled=True)  61.6 us
    unnamed x13, local copies, waits for them, and re-layouts  50.3 us
    reduce_scatter x1, waiting for transfers between devices, body(): lax.psum_scatter(term.reshape(pair_rows * lax.axis_size('gx'), -1), 'gx',...  46.9 us
    dot_general x1, matrix products, body(): jnp.einsum('tdxpky,pkz->tdxyz', cells_y, z_inverse, preferred_element_typ...  30.8 us
    dot_general x1, matrix products, body(): jnp.einsum('tcxyz,cd->tdxyz', plume_state, pointwise_weight, preferred_el...  11.3 us
    unnamed x3, waiting for transfers between devices  9.98 us
    all_gather x1, local copies, waits for them, and re-layouts, body(): lax.all_gather(mixed_modes, 'gx', axis=0, tiled=True)  7.43 us
    reshape x1, local copies, waits for them, and re-layouts, body(): spectral = spectral_weight.reshape(pair_rows, MX, 2, channels, channels)  6.06 us
  transfers between devices with their start and end apart: 2, of which 2 were waited for; matrix products, arithmetic and copies ran while one was open for 7% of the time, Pallas kernels for 0%

commit v1 on v0

v1 whole, which is shorter than its diff:
```python
import functools
import math

import jax
import jax.numpy as jnp
import ml_dtypes
import numpy as np
from jax import lax
from jax.experimental import pallas as pl
from jax.experimental.pallas import tpu as pltpu
from jax.sharding import PartitionSpec as P

MX = 24
MY = 16
MZ = 16
LANES = 128
TILE = 16
MESH = pl.DeviceIdType.MESH
F32 = jnp.float32
BF16 = jnp.bfloat16


def retained(kept, length):
    indices = np.arange(kept)
    return np.where(indices < kept // 2, indices, length - kept + indices)


def phases(freq_ids, positions, length):
    product = freq_ids[:, None] * positions[None, :] % length
    return np.float32(2.0 * math.pi / length) * product.astype(np.float32)


def forward_table(freq_ids, positions, length):
    angles = phases(freq_ids, positions, length).T
    cosine, sine = np.cos(angles), np.sin(angles)
    return np.stack([np.stack([cosine, -sine], 1), np.stack([sine, cosine], 1)], 1)


def inverse_table(freq_ids, positions, length):
    angles = phases(freq_ids, positions, length)
    cosine, sine = np.cos(angles), np.sin(angles)
    return np.stack([np.stack([cosine, sine], 1), np.stack([-sine, cosine], 1)], 0)


def up(value, step):
    return -(-value // step) * step


def pad_last(table, width):
    return np.pad(table, [(0, 0)] * (table.ndim - 1) + [(0, width - table.shape[-1])])


def tables(n_gx, n_gy, rows_x, rows_y, depth, pair_rows, group):
    length_x, length_y = n_gx * rows_x, n_gy * rows_y
    blocks = MY // pair_rows
    lanes_l = up(pair_rows * MX, LANES)
    angles = phases(np.arange(MZ), np.arange(depth), depth)
    z_forward = np.concatenate([np.cos(angles), -np.sin(angles)], 0)

    y_ids, x_ids = retained(MY, length_y), retained(MX, length_x)
    eye_x, eye_m = np.eye(rows_x), np.eye(pair_rows)
    fy = forward_table(y_ids, np.arange(length_y), length_y)
    fy = fy.reshape(n_gy, rows_y, 2, 2, blocks, pair_rows)
    y_forward = np.einsum("gypqbm,xw->gpxybwqm", fy, eye_x)
    y_forward = y_forward.reshape(n_gy, 2 * rows_x * rows_y, blocks, -1)
    y_forward = pad_last(y_forward, LANES).reshape(n_gy, 2 * rows_x * rows_y, blocks * LANES)

    fx = forward_table(x_ids, np.arange(length_x), length_x).reshape(n_gx, rows_x, 2, 2, MX)
    x_forward = np.einsum("ixqpk,mn->pnkixqm", fx, eye_m).reshape(2, pair_rows * MX, n_gx, -1)
    x_forward = pad_last(x_forward, LANES).reshape(2, pair_rows * MX, n_gx * LANES)
    x_forward = np.pad(x_forward, [(0, 0), (0, lanes_l - pair_rows * MX), (0, 0)])
    x_forward = x_forward.reshape(2 * lanes_l, n_gx * LANES).T

    ix = inverse_table(x_ids, np.arange(length_x), length_x).reshape(2, MX, 2, n_gx, rows_x)
    x_back = np.einsum("qkpix,mn->qnkixpm", ix, eye_m).reshape(2, pair_rows * MX, n_gx, -1)
    x_back = pad_last(x_back, LANES).reshape(2, pair_rows * MX, n_gx * LANES)
    x_back = np.pad(x_back, [(0, 0), (0, lanes_l - pair_rows * MX), (0, 0)])
    x_back = x_back.reshape(2 * lanes_l, n_gx * LANES)

    iy = inverse_table(y_ids, np.arange(length_y), length_y)
    iy = iy.reshape(2, blocks, pair_rows, 2, n_gy, rows_y)
    y_back = np.einsum("qbmpgy,xw->gxpybwqm", iy, eye_x)
    y_back = y_back.reshape(n_gy, rows_x, 2 * rows_y, blocks, -1)
    y_back = pad_last(y_back, LANES).reshape(n_gy, rows_x, 2 * rows_y, blocks * LANES)

    doubling = np.where(np.arange(MZ) == 0, 1.0, 2.0)[:, None]
    iz = np.stack([doubling * np.cos(angles), -doubling * np.sin(angles)], 0)
    iz = iz.astype(ml_dtypes.bfloat16).astype(np.float32) / (length_x * length_y * depth)
    z_back = np.einsum("pkz,jh->pjkhz", iz, np.eye(group))
    z_back = z_back.reshape(2 * group * MZ, group * depth)
    return [
        jnp.asarray(np.ascontiguousarray(t, dtype=np.float32).astype(ml_dtypes.bfloat16))
        for t in (z_forward, y_forward, x_forward, x_back, y_back, z_back)
    ]


def dot(a, b):
    return jnp.dot(a, b, preferred_element_type=F32)


def dot_lanes(a, b):
    return lax.dot_general(a, b, (((1,), (1,)), ((), ())), preferred_element_type=F32)


def forward_kernel(fields, steps, plume, z_forward, y_forward, out, rows):
    step = pl.program_id(0)
    half = lax.axis_index("gy")
    group = plume.shape[0]
    blocks = y_forward.shape[2] // LANES
    parts = []
    for j in range(group):
        modes = dot_lanes(z_forward[...], plume[j]).astype(BF16)
        parts.append(jnp.concatenate([modes[:MZ], modes[MZ:]], axis=1))
    terms = dot(jnp.concatenate(parts, axis=0), y_forward[half])
    size = group * MZ
    for block in range(blocks):
        rows[block, pl.ds(pl.multiple_of(step * size, size), size), :] = terms[
            :, block * LANES : (block + 1) * LANES
        ]

    @pl.when(step == steps - 1)
    def _():
        slot_rows = out.shape[1]
        if slot_rows > fields:
            extra = (slot_rows - fields) * MZ
            rows[:, pl.ds(fields * MZ, extra), :] = jnp.zeros((blocks, extra, LANES), F32)
        for kz in range(MZ):
            for block in range(blocks):
                out[kz * blocks + block] = rows[
                    block, pl.ds(kz, slot_rows, stride=MZ), :
                ].astype(BF16)


def each(count, one):
    if count <= 16:
        for s in range(1, count):
            one(s)
    else:
        lax.fori_loop(1, count, lambda s, _: (one(s), 0)[1], 0)


def modes_kernel(
    n_gx, n_gy, snapshots, channels,
    sent, weights, x_forward, x_back, out,
    landed, back, going, mixers, pairs, mixed, order,
    send_one, recv_one, send_two, recv_two,
):
    count = n_gx * n_gy
    my_x, my_y = lax.axis_index("gx"), lax.axis_index("gy")
    me = my_y * n_gx + my_x
    fields = snapshots * channels
    wide = mixers.shape[1]

    def device(index):
        return {"gx": lax.rem(index, n_gx), "gy": lax.div(index, n_gx)}

    barrier = pltpu.get_barrier_semaphore()

    def greet(s):
        peer = lax.rem(me + s, count)
        pl.semaphore_signal(barrier, inc=1, device_id=device(peer), device_id_type=MESH)

    each(count, greet)
    pl.semaphore_wait(barrier, count - 1)

    def first(s, at):
        peer = lax.rem(me + s, count)
        return pltpu.make_async_remote_copy(
            src_ref=sent.at[peer], dst_ref=landed.at[at],
            send_sem=send_one.at[s], recv_sem=recv_one.at[s],
            device_id=device(peer), device_id_type=MESH,
        )

    def second(s, at):
        peer = lax.rem(me + s, count)
        return pltpu.make_async_remote_copy(
            src_ref=going.at[lax.rem(peer, n_gx)], dst_ref=back.at[at],
            send_sem=send_two.at[s], recv_sem=recv_two.at[s],
            device_id=device(peer), device_id_type=MESH,
        )

    def source(s):
        return lax.rem(me + count - s, count)

    each(count, lambda s: first(s, me).start())
    landed[me] = sent[me]

    length = weights.shape[1]
    for at in range(0, length, LANES):
        width = min(LANES, length - at)
        chunk = weights[:, pl.ds(at, width)].astype(F32)
        if width < LANES:
            chunk = jnp.concatenate([chunk, jnp.zeros((wide, LANES - width), F32)], axis=1)
        mixers[pl.ds(at, LANES), :] = chunk.T

    each(count, lambda s: first(s, source(s)).wait_recv())
    summed = []
    for i in range(n_gx):
        total = landed[i].astype(F32)
        for g in range(1, n_gy):
            total += landed[g * n_gx + i].astype(F32)
        summed.append(total.astype(BF16))
    pairs[...] = dot(jnp.concatenate(summed, axis=1), x_forward[...]).astype(BF16).astype(F32)

    square = channels * channels
    mixed[...] = jnp.zeros_like(mixed)
    for t in range(snapshots):
        real = jnp.zeros((channels, wide), F32)
        imag = jnp.zeros((channels, wide), F32)
        for c in range(channels):
            mode_real = pairs[pl.ds(t * channels + c, 1), pl.ds(0, wide)]
            mode_imag = pairs[pl.ds(t * channels + c, 1), pl.ds(wide, wide)]
            weight_real = mixers[pl.ds(c * channels, channels), :]
            weight_imag = mixers[pl.ds(square + c * channels, channels), :]
            real += mode_real * weight_real - mode_imag * weight_imag
            imag += mode_real * weight_imag + mode_imag * weight_real
        mixed[pl.ds(t * channels, channels), pl.ds(0, wide)] = real
        mixed[pl.ds(t * channels, channels), pl.ds(wide, wide)] = imag
    cells = dot(mixed[...].astype(BF16), x_back[...]).astype(BF16)
    for i in range(n_gx):
        going[i] = cells[:, i * LANES : (i + 1) * LANES]

    each(count, lambda s: second(s, me).start())
    back[me] = going[my_x]
    each(count, lambda s: second(s, source(s)).wait_recv())
    blocks = count // MZ
    for kz in range(MZ):
        for block in range(blocks):
            order[block, pl.ds(kz, fields, stride=MZ), :] = back[kz * blocks + block].astype(
                F32
            )[:fields]
    for block in range(blocks):
        out[:, pl.ds(block * LANES, LANES)] = order[block].astype(BF16)
    each(count, lambda s: first(s, me).wait_send())
    each(count, lambda s: second(s, me).wait_send())


def inverse_kernel(
    snapshots, channels, plume, cells, y_back, z_back, pointwise, bias, out, spectral
):
    x = pl.program_id(0)
    half = lax.axis_index("gy")
    fields, _, rows_y, depth = plume.shape
    group = z_back.shape[1] // depth
    table = y_back[half, x]
    grid_modes = dot_lanes(table, cells[...]).astype(BF16)
    real, imag = grid_modes[:rows_y], grid_modes[rows_y:]
    width = group * MZ
    for g in range(fields // group):
        both = jnp.concatenate(
            [real[:, g * width : (g + 1) * width], imag[:, g * width : (g + 1) * width]], axis=1
        )
        values = dot(both, z_back[...])
        for j in range(group):
            spectral[g * group + j] = values[:, j * depth : (j + 1) * depth]

    for t in range(snapshots):
        def strip(i, _, t=t):
            base = pl.multiple_of(i * 2 * TILE, 2 * TILE)
            fld = pl.ds(t * channels, channels)
            block = plume[fld, 0, pl.ds(base, 2 * TILE), :]
            pair = jnp.concatenate(
                [
                    block[:, :TILE].reshape(channels * TILE, depth),
                    block[:, TILE:].reshape(channels * TILE, depth),
                ],
                axis=1,
            )
            local = dot(pointwise[...], pair)
            for h in range(2):
                rows = pl.ds(base + h * TILE, TILE)
                value = local[:, h * depth : (h + 1) * depth].reshape(channels, TILE, depth)
                value = value + spectral[fld, rows, :] + bias[...]
                value = 0.5 * value * (1.0 + lax.erf(value * math.sqrt(0.5)))
                out[fld, 0, rows, :] = value.astype(BF16)
            return 0

        lax.fori_loop(0, rows_y // (2 * TILE), strip, 0)


def body(n_gx, n_gy, plume_state, spectral_weight, pointwise_weight, channel_bias):
    snapshots, channels, rows_x, rows_y, depth = plume_state.shape
    fields = snapshots * channels
    pair_rows = spectral_weight.shape[1]
    count = n_gx * n_gy
    blocks = MY // pair_rows
    group = LANES // MZ
    slot = up(fields, TILE)
    wide = up(pair_rows * MX, LANES)
    z_forward, y_forward, x_forward, x_back, y_back, z_back = tables(
        n_gx, n_gy, rows_x, rows_y, depth, pair_rows, group
    )
    whole = pl.BlockSpec(memory_space=pltpu.VMEM)
    limit = 50 * 2**20
    steps = fields // group
    sent = pl.pallas_call(
        functools.partial(forward_kernel, fields, steps),
        grid=(steps,),
        out_shape=jax.ShapeDtypeStruct((count, slot, LANES), BF16),
        in_specs=[
            pl.BlockSpec((group, rows_x * rows_y, depth), lambda g: (g, 0, 0)),
            whole,
            whole,
        ],
        out_specs=pl.BlockSpec((count, slot, LANES), lambda g: (0, 0, 0)),
        scratch_shapes=[pltpu.VMEM((blocks, slot * MZ, LANES), F32)],
        compiler_params=pltpu.CompilerParams(vmem_limit_bytes=limit),
        name="forward",
    )(plume_state.reshape(fields, rows_x * rows_y, depth), z_forward, y_forward)

    weights = spectral_weight.reshape(pair_rows * MX, -1)
    weights = jnp.pad(weights, [(0, wide - pair_rows * MX), (0, 0)])
    sems = pltpu.SemaphoreType.DMA((count,))
    cells = pl.pallas_call(
        functools.partial(modes_kernel, n_gx, n_gy, snapshots, channels),
        out_shape=jax.ShapeDtypeStruct((fields * MZ, blocks * LANES), BF16),
        in_specs=[whole] * 4,
        out_specs=whole,
        scratch_shapes=[
            pltpu.VMEM((count, slot, LANES), BF16),
            pltpu.VMEM((count, slot, LANES), BF16),
            pltpu.VMEM((n_gx, slot, LANES), BF16),
            pltpu.VMEM((up(weights.shape[1], LANES), wide), F32),
            pltpu.VMEM((slot, 2 * wide), F32),
            pltpu.VMEM((slot, 2 * wide), F32),
            pltpu.VMEM((blocks, fields * MZ, LANES), F32),
            sems, sems, sems, sems,
        ],
        compiler_params=pltpu.CompilerParams(
            vmem_limit_bytes=limit, collective_id=0, has_side_effects=True
        ),
        name="modes",
    )(sent, weights, x_forward, x_back)

    pointwise = (
        pointwise_weight.T[:, None, :, None] * jnp.eye(TILE, dtype=BF16)[None, :, None, :]
    ).reshape(channels * TILE, channels * TILE)
    bias = jnp.broadcast_to(channel_bias[:, None, None], (channels, 1, depth))
    state = plume_state.reshape(fields, rows_x, rows_y, depth)
    slab = pl.BlockSpec((fields, 1, rows_y, depth), lambda x: (0, x, 0, 0))
    result = pl.pallas_call(
        functools.partial(inverse_kernel, snapshots, channels),
        grid=(rows_x,),
        out_shape=jax.ShapeDtypeStruct(state.shape, BF16),
        in_specs=[slab] + [whole] * 5,
        out_specs=slab,
        scratch_shapes=[pltpu.VMEM((fields, rows_y, depth), F32)],
        compiler_params=pltpu.CompilerParams(vmem_limit_bytes=limit),
        name="inverse",
    )(state, cells, y_back, z_back, pointwise, bias)
    return result.reshape(plume_state.shape)


def solution(mesh):
    placed = (P("groups", None, "gx", "gy", None), P("gy", "gx", None, None), P(), P())
    return jax.shard_map(
        functools.partial(body, mesh.shape["gx"], mesh.shape["gy"]),
        mesh=mesh,
        in_specs=placed,
        out_specs=P("groups", None, "gx", "gy", None),
        check_vma=False,
    )
```

time: 263 us -> 46 us (0.17)
  blocking collectives: 63.5 us -> 0 us
  local copies, waits for them, and re-layouts: 65.8 us -> 4.47 us
  matrix products: 61.3 us -> 0 us
  waiting for transfers between devices: 56.8 us -> 0 us
  Pallas kernels: 0 us -> 40.8 us
  between operations: 13.8 us -> 0.1 us
    all_gather x2 -> x0, blocking collectives: 63.5 us -> none  [the longest x1 61.6 us: body(): lax.all_gather(mixed_modes, 'gx', axis=0, tiled=True)]
    dot_general x10 -> x0, matrix products: 61.3 us -> none  [the longest x1 30.8 us: body(): jnp.einsum('tdxpky,pkz->tdxyz', cells_y, z_inverse, preferred_element_typ...]
    unnamed x13 -> x12, local copies, waits for them, and re-layouts: 50.3 us -> 1.76 us
    reduce_scatter x1 -> x0, waiting for transfers between devices: 46.9 us -> none  [body(): lax.psum_scatter(term.reshape(pair_rows * lax.axis_size('gx'), -1), 'gx',...]
    pallas_call x0 -> x3, Pallas kernels: none -> 40.8 us  [the longest x1 21.2 us: body(): pl.pallas_call(functools.partial(modes_kernel, n_gx, n_gy, snapshots, cha...]
    unnamed x3 -> x0, waiting for transfers between devices: 9.98 us -> none
    all_gather x2 -> x0, local copies, waits for them, and re-layouts: 7.6 us -> none  [the longest x1 7.43 us: body(): lax.all_gather(mixed_modes, 'gx', axis=0, tiled=True)]
    reshape x3 -> x0, local copies, waits for them, and re-layouts: 7.38 us -> none  [the longest x1 6.06 us: body(): spectral = spectral_weight.reshape(pair_rows, MX, 2, channels, channels)]
  transfers between devices with their start and end apart: 2 -> 0, of which waited for: 2 -> 0; matrix products, arithmetic and copies ran while one was open for 7% -> 0% of each run, Pallas kernels for 0% -> 0%
where the time goes in v1:
time: 46 us; the launch traced here: 45.6 us
  Pallas kernels  40.8 us (89%)
  local copies, waits for them, and re-layouts  4.47 us (10%)
    pallas_call x1, Pallas kernels, body(): pl.pallas_call(functools.partial(modes_kernel, n_gx, n_gy, snapshots, cha...  21.2 us
    pallas_call x1, Pallas kernels, body(): pl.pallas_call(functools.partial(inverse_kernel, snapshots, channels), gr...  13.7 us
    pallas_call x1, Pallas kernels, body(): pl.pallas_call(functools.partial(forward_kernel, fields, steps), grid=(st...  5.86 us
    unnamed x12, local copies, waits for them, and re-layouts  1.76 us
    mul x1, local copies, waits for them, and re-layouts, body(): pointwise_weight.T[:, None, :, None]  1.2 us

profile of v1, /device:TPU:0, one launch (start us, length us, event | category | flops | bytes accessed | tf_op | source)
XLA Modules:
  0.0 45.6 jit_solution(12801193790116131657)
XLA Ops:
  0.0 0.8 %copy.12 = bf16[20,20]{1,0:T(8,128)(2,1)S(1)} copy(bf16[20,20]{0,1:T(8,128)(2,1)} %bitcast.8) | data formatting | bytes 1600 | tf_op jit(solution)/shard_map/transpose | solution.py:336
  0.8 0.7 %broadcast_in_dim.2.bias = f32[20,1,128]{2,1,0:T(1,128)S(1)} broadcast(f32[20]{0:T(128)} %param.13), dimensions={0} | broadcast | bytes 10320 | tf_op jit(solution)/shard_map/broadcast_in_dim | solution.py:338
  1.5 0.0 copy-start.4
  1.5 1.0 %copy-done.4 = bf16[2,1024,128]{2,1,0:T(8,128)(2,1)S(1)} copy-done((bf16[2,1024,128]{2,1,0:T(8,128)(2,1)S(1)}, bf16[2,1024,128]{2,1,0:T(8,128)(2,1)}, u32[]{:S(2)}) %copy-start.4) | copy-done | bytes 524312
  2.6 0.0 copy-start.5
  2.6 0.7 %copy-done.5 = bf16[32,128]{1,0:T(8,128)(2,1)S(1)} copy-done((bf16[32,128]{1,0:T(8,128)(2,1)S(1)}, bf16[32,128]{1,0:T(8,128)(2,1)}, u32[]{:S(2)}) %copy-start.5) | copy-done | bytes 8216
  3.3 0.0 copy-start
  3.3 0.0 copy-start.1
  3.3 5.9 %forward.1.sent = bf16[16,48,128]{2,1,0:T(8,128)(2,1)S(1)} custom-call(bf16[40,512,128]{2,1,0:T(8,128)(2,1)} %bitcast.6, bf16[32,128]{1,0:T(8,128)(2,1)S(1)} %copy-done.5, bf16[2,1024,128]{2,1,0:T(8,128)(2,1)S(1)} %copy-done.4), custom_call_target="tpu_custom_call" | custom-call | tf_op jit(solution)/shard_map/forward/pallas_call | solution.py:296
  9.2 0.0 copy-done
  9.2 0.0 copy-done.1
  9.2 21.2 %modes.1.cells = bf16[640,128]{1,0:T(8,128)(2,1)S(1)} custom-call(bf16[16,48,128]{2,1,0:T(8,128)(2,1)S(1)} %forward.1.sent, bf16[384,800]{1,0:T(8,128)(2,1)S(1)} %bitcast.5, bf16[1024,768]{1,0:T(8,128)(2,1)S(1)} %copy-done, bf16[768,1024]{1,0:T(8,128)(2,1)} %constant.16.clone.x_back), custom_call_target="tpu_custom_call" | custom-call | tf_op jit(solution)/shard_map/modes/pallas_call | solution.py:314
  30.4 0.0 copy-start.2
  30.4 0.0 copy-start.3
  30.4 0.2 broadcast_multiply_fusion
  30.6 1.2 %mul.20.pointwise = bf16[320,320]{1,0:T(8,128)(2,1)S(1)} reshape(bf16[20,16,20,16]{3,2,1,0:T(8,128)(2,1)S(1)} %broadcast_multiply_fusion) | data formatting | bytes 409600 | tf_op jit(solution)/shard_map/mul | solution.py:336
  31.8 0.0 copy-done.2
  31.8 0.0 copy-done.3
  31.8 13.7 %inverse.1 = bf16[40,4,128,128]{3,2,1,0:T(8,128)(2,1)} custom-call(bf16[40,4,128,128]{3,2,1,0:T(8,128)(2,1)} %bitcast.7, bf16[640,128]{1,0:T(8,128)(2,1)S(1)} %modes.1.cells, bf16[2,4,256,128]{3,2,1,0:T(8,128)(2,1)S(1)} %copy-done.3, bf16[256,1024]{1,0:T(8,128)(2,1)S(1)} %copy-done.2, bf16[320,320]{1,0:T(8,128)(2,1)S(1)} %mul.20.pointwise, ...), custom_call_target="tpu_custom_call" | custom-call | tf_op jit(solution)/shard_map/inverse/pallas_call | solution.py:341
  (1 shorter events, 0.0 us)
Async XLA Ops:
  1.5 1.0 %copy-start.4 = (bf16[2,1024,128]{2,1,0:T(8,128)(2,1)S(1)}, bf16[2,1024,128]{2,1,0:T(8,128)(2,1)}, u32[]{:S(2)}) copy-start(bf16[2,1024,128]{2,1,0:T(8,128)(2,1)} %constant.14.clone.y_forward) | copy-start | bytes 1572868
  2.6 0.7 %copy-start.5 = (bf16[32,128]{1,0:T(8,128)(2,1)S(1)}, bf16[32,128]{1,0:T(8,128)(2,1)}, u32[]{:S(2)}) copy-start(bf16[32,128]{1,0:T(8,128)(2,1)} %constant.6.clone.z_forward) | copy-start | bytes 24580
  3.3 5.9 %copy-start = (bf16[1024,768]{1,0:T(8,128)(2,1)S(1)}, bf16[1024,768]{1,0:T(8,128)(2,1)}, u32[]{:S(2)}) copy-start(bf16[1024,768]{1,0:T(8,128)(2,1)} %constant.15.clone.x_forward) | copy-start | bytes 4718596
  3.3 5.9 %copy-start.1 = (bf16[1,16,24,800]{3,2,1,0:T(8,128)(2,1)S(1)}, bf16[1,16,24,800]{3,2,1,0:T(8,128)(2,1)}, u32[]{:S(2)}) copy-start(bf16[1,16,24,800]{3,2,1,0:T(8,128)(2,1)} %param.11) | copy-start | bytes 1843204
  30.4 1.4 %copy-start.2 = (bf16[256,1024]{1,0:T(8,128)(2,1)S(1)}, bf16[256,1024]{1,0:T(8,128)(2,1)}, u32[]{:S(2)}) copy-start(bf16[256,1024]{1,0:T(8,128)(2,1)} %constant.18.clone.z_back) | copy-start | bytes 1572868
  30.4 1.4 %copy-start.3 = (bf16[2,4,256,128]{3,2,1,0:T(8,128)(2,1)S(1)}, bf16[2,4,256,128]{3,2,1,0:T(8,128)(2,1)}, u32[]{:S(2)}) copy-start(bf16[2,4,256,128]{3,2,1,0:T(8,128)(2,1)} %constant.17.clone.y_back) | copy-start | bytes 1572868

commit v2 on v1

--- a/solution.py
+++ b/solution.py
@@ -79,9 +79,9 @@
 
     iy = inverse_table(y_ids, np.arange(length_y), length_y)
     iy = iy.reshape(2, blocks, pair_rows, 2, n_gy, rows_y)
-    y_back = np.einsum("qbmpgy,xw->gxpybwqm", iy, eye_x)
-    y_back = y_back.reshape(n_gy, rows_x, 2 * rows_y, blocks, -1)
-    y_back = pad_last(y_back, LANES).reshape(n_gy, rows_x, 2 * rows_y, blocks * LANES)
+    y_back = np.einsum("qbmpgy,xw->gpxybwqm", iy, eye_x)
+    y_back = y_back.reshape(n_gy, 2, rows_x * rows_y, blocks, -1)
+    y_back = pad_last(y_back, LANES).reshape(n_gy, 2, rows_x * rows_y, blocks * LANES)
 
     doubling = np.where(np.arange(MZ) == 0, 1.0, 2.0)[:, None]
     iz = np.stack([doubling * np.cos(angles), -doubling * np.sin(angles)], 0)
@@ -102,35 +102,6 @@
     return lax.dot_general(a, b, (((1,), (1,)), ((), ())), preferred_element_type=F32)
 
 
-def forward_kernel(fields, steps, plume, z_forward, y_forward, out, rows):
-    step = pl.program_id(0)
-    half = lax.axis_index("gy")
-    group = plume.shape[0]
-    blocks = y_forward.shape[2] // LANES
-    parts = []
-    for j in range(group):
-        modes = dot_lanes(z_forward[...], plume[j]).astype(BF16)
-        parts.append(jnp.concatenate([modes[:MZ], modes[MZ:]], axis=1))
-    terms = dot(jnp.concatenate(parts, axis=0), y_forward[half])
-    size = group * MZ
-    for block in range(blocks):
-        rows[block, pl.ds(pl.multiple_of(step * size, size), size), :] = terms[
-            :, block * LANES : (block + 1) * LANES
-        ]
-
-    @pl.when(step == steps - 1)
-    def _():
-        slot_rows = out.shape[1]
-        if slot_rows > fields:
-            extra = (slot_rows - fields) * MZ
-            rows[:, pl.ds(fields * MZ, extra), :] = jnp.zeros((blocks, extra, LANES), F32)
-        for kz in range(MZ):
-            for block in range(blocks):
-                out[kz * blocks + block] = rows[
-                    block, pl.ds(kz, slot_rows, stride=MZ), :
-                ].astype(BF16)
-
-
 def each(count, one):
     if count <= 16:
         for s in range(1, count):
@@ -140,19 +111,39 @@
 
 
 def modes_kernel(
-    n_gx, n_gy, snapshots, channels,
-    sent, weights, x_forward, x_back, out,
-    landed, back, going, mixers, pairs, mixed, order,
-    send_one, recv_one, send_two, recv_two,
+    n_gx, n_gy, snapshots, channels, group,
+    plume_in, z_forward, y_forward, weights_in, x_forward_in, x_back_in, pointwise, spread,
+    out, local_out,
+    plume, weights, x_forward, x_back, rows, sent,
+    landed, back, going, mixers, pairs, mixed, order, local, kron,
+    in_sem, table_sem, local_sem, send_one, recv_one, send_two, recv_two,
 ):
     count = n_gx * n_gy
     my_x, my_y = lax.axis_index("gx"), lax.axis_index("gy")
     me = my_y * n_gx + my_x
     fields = snapshots * channels
     wide = mixers.shape[1]
+    blocks = count // MZ
+    slot_rows = sent.shape[1]
+    steps = fields // group
 
     def device(index):
         return {"gx": lax.rem(index, n_gx), "gy": lax.div(index, n_gx)}
+
+    def chunk_in(g):
+        part = pl.ds(g * group, group)
+        return pltpu.make_async_copy(plume_in.at[part], plume.at[part], in_sem.at[g])
+
+    for g in range(steps):
+        chunk_in(g).start()
+    held = [
+        pltpu.make_async_copy(src, dst, table_sem.at[i])
+        for i, (src, dst) in enumerate(
+            [(weights_in, weights), (x_forward_in, x_forward), (x_back_in, x_back)]
+        )
+    ]
+    for copy in held:
+        copy.start()
 
     barrier = pltpu.get_barrier_semaphore()
 
@@ -161,7 +152,61 @@
         pl.semaphore_signal(barrier, inc=1, device_id=device(peer), device_id_type=MESH)
 
     each(count, greet)
+    size = channels * TILE
+    scaled = dot_lanes(dot_lanes(spread[...], pointwise[...]).astype(BF16), spread[...])
+    at_row = lax.broadcasted_iota(jnp.int32, (size, size), 0) % TILE
+    at_column = lax.broadcasted_iota(jnp.int32, (size, size), 1) % TILE
+    kron[...] = jnp.where(at_row == at_column, scaled, 0.0).astype(BF16)
+
+    rows[:, pl.ds(fields * MZ, (slot_rows - fields) * MZ), :] = jnp.zeros(
+        (blocks, (slot_rows - fields) * MZ, LANES), F32
+    )
+    for g in range(steps):
+        chunk_in(g).wait()
+        parts = []
+        for j in range(group):
+            modes = dot_lanes(z_forward[...], plume[g * group + j]).astype(BF16)
+            parts.append(jnp.concatenate([modes[:MZ], modes[MZ:]], axis=1))
+        terms = dot(jnp.concatenate(parts, axis=0), y_forward[my_y])
+        for block in range(blocks):
+            rows[block, pl.ds(g * group * MZ, group * MZ), :] = terms[
+                :, block * LANES : (block + 1) * LANES
+            ]
+    for kz in range(MZ):
+        for block in range(blocks):
+            sent[kz * blocks + block] = rows[block, pl.ds(kz, slot_rows, stride=MZ), :].astype(
+                BF16
+            )
     pl.semaphore_wait(barrier, count - 1)
+
+    depth = plume.shape[2]
+
+    def pointwise_of(t):
+        fld = pl.ds(t * channels, channels)
+
+        def strip(i, _):
+            base = pl.multiple_of(i * 2 * TILE, 2 * TILE)
+            block = plume[fld, pl.ds(base, 2 * TILE), :]
+            pair = jnp.concatenate(
+                [
+                    block[:, :TILE].reshape(size, depth),
+                    block[:, TILE:].reshape(size, depth),
+                ],
+                axis=1,
+            )
+            value = dot(kron[...], pair)
+            for h in range(2):
+                local[fld, pl.ds(base + h * TILE, TILE), :] = value[
+                    :, h * depth : (h + 1) * depth
+                ].reshape(channels, TILE, depth)
+            return 0
+
+        lax.fori_loop(0, plume.shape[1] // (2 * TILE), strip, 0)
+        local_copy(t).start()
+
+    def local_copy(t):
+        fld = pl.ds(t * channels, channels)
+        return pltpu.make_async_copy(local.at[fld], local_out.at[fld], local_sem.at[t])
 
     def first(s, at):
         peer = lax.rem(me + s, count)
@@ -185,6 +230,8 @@
     each(count, lambda s: first(s, me).start())
     landed[me] = sent[me]
 
+    for copy in held:
+        copy.wait()
     length = weights.shape[1]
     for at in range(0, length, LANES):
         width = min(LANES, length - at)
@@ -192,6 +239,7 @@
         if width < LANES:
             chunk = jnp.concatenate([chunk, jnp.zeros((wide, LANES - width), F32)], axis=1)
         mixers[pl.ds(at, LANES), :] = chunk.T
+    pointwise_of(0)
 
     each(count, lambda s: first(s, source(s)).wait_recv())
     summed = []
@@ -222,8 +270,9 @@
 
     each(count, lambda s: second(s, me).start())
     back[me] = going[my_x]
+    for t in range(1, snapshots):
+        pointwise_of(t)
     each(count, lambda s: second(s, source(s)).wait_recv())
-    blocks = count // MZ
     for kz in range(MZ):
         for block in range(blocks):
             order[block, pl.ds(kz, fields, stride=MZ), :] = back[kz * blocks + block].astype(
@@ -233,54 +282,44 @@
         out[:, pl.ds(block * LANES, LANES)] = order[block].astype(BF16)
     each(count, lambda s: first(s, me).wait_send())
     each(count, lambda s: second(s, me).wait_send())
-
-
-def inverse_kernel(
-    snapshots, channels, plume, cells, y_back, z_back, pointwise, bias, out, spectral
-):
-    x = pl.program_id(0)
+    for t in range(snapshots):
+        local_copy(t).wait()
+
+
+E = (
+    0.797884268412902, 0.03633414910206053, -3.3026689185494805e-05, -5.527339041578515e-05,
+    3.974071266817981e-06, -1.3378326030725087e-07, 1.8139279592266355e-09,
+)
+
+
+def gelu(x):
+    square = jnp.minimum(x * x, 30.25)
+    series = jnp.full_like(x, E[-1])
+    for term in E[-2::-1]:
+        series = series * square + term
+    half = 0.5 * x
+    return half + half * jnp.tanh(x * series)
+
+
+def inverse_kernel(channels, local, cells, y_back, z_back, bias, out):
+    g = pl.program_id(0)
     half = lax.axis_index("gy")
-    fields, _, rows_y, depth = plume.shape
-    group = z_back.shape[1] // depth
-    table = y_back[half, x]
-    grid_modes = dot_lanes(table, cells[...]).astype(BF16)
-    real, imag = grid_modes[:rows_y], grid_modes[rows_y:]
-    width = group * MZ
-    for g in range(fields // group):
-        both = jnp.concatenate(
-            [real[:, g * width : (g + 1) * width], imag[:, g * width : (g + 1) * width]], axis=1
-        )
-        values = dot(both, z_back[...])
-        for j in range(group):
-            spectral[g * group + j] = values[:, j * depth : (j + 1) * depth]
-
-    for t in range(snapshots):
-        def strip(i, _, t=t):
-            base = pl.multiple_of(i * 2 * TILE, 2 * TILE)
-            fld = pl.ds(t * channels, channels)
-            block = plume[fld, 0, pl.ds(base, 2 * TILE), :]
-            pair = jnp.concatenate(
-                [
-                    block[:, :TILE].reshape(channels * TILE, depth),
-                    block[:, TILE:].reshape(channels * TILE, depth),
-                ],
-                axis=1,
-            )
-            local = dot(pointwise[...], pair)
-            for h in range(2):
-                rows = pl.ds(base + h * TILE, TILE)
-                value = local[:, h * depth : (h + 1) * depth].reshape(channels, TILE, depth)
-                value = value + spectral[fld, rows, :] + bias[...]
-                value = 0.5 * value * (1.0 + lax.erf(value * math.sqrt(0.5)))
-                out[fld, 0, rows, :] = value.astype(BF16)
-            return 0
-
-        lax.fori_loop(0, rows_y // (2 * TILE), strip, 0)
+    group, _, depth = local.shape
+    both = jnp.concatenate(
+        [dot_lanes(y_back[half, p], cells[...]).astype(BF16) for p in range(2)], axis=1
+    )
+    for j in range(0, group, 2):
+        values = dot(both, z_back[:, j * depth : (j + 2) * depth])
+        for h in range(2):
+            level = bias[lax.rem(g * group + j + h, channels)]
+            value = values[:, h * depth : (h + 1) * depth] + local[j + h] + level
+            out[j + h] = gelu(value).astype(BF16)
 
 
 def body(n_gx, n_gy, plume_state, spectral_weight, pointwise_weight, channel_bias):
     snapshots, channels, rows_x, rows_y, depth = plume_state.shape
     fields = snapshots * channels
+    cells_xy = rows_x * rows_y
     pair_rows = spectral_weight.shape[1]
     count = n_gx * n_gy
     blocks = MY // pair_rows
@@ -290,33 +329,30 @@
     z_forward, y_forward, x_forward, x_back, y_back, z_back = tables(
         n_gx, n_gy, rows_x, rows_y, depth, pair_rows, group
     )
+    spread = jnp.asarray(np.repeat(np.eye(channels), TILE, axis=0).astype(ml_dtypes.bfloat16))
     whole = pl.BlockSpec(memory_space=pltpu.VMEM)
-    limit = 50 * 2**20
+    anywhere = pl.BlockSpec(memory_space=pl.ANY)
+    limit = 60 * 2**20
     steps = fields // group
-    sent = pl.pallas_call(
-        functools.partial(forward_kernel, fields, steps),
-        grid=(steps,),
-        out_shape=jax.ShapeDtypeStruct((count, slot, LANES), BF16),
-        in_specs=[
-            pl.BlockSpec((group, rows_x * rows_y, depth), lambda g: (g, 0, 0)),
-            whole,
-            whole,
-        ],
-        out_specs=pl.BlockSpec((count, slot, LANES), lambda g: (0, 0, 0)),
-        scratch_shapes=[pltpu.VMEM((blocks, slot * MZ, LANES), F32)],
-        compiler_params=pltpu.CompilerParams(vmem_limit_bytes=limit),
-        name="forward",
-    )(plume_state.reshape(fields, rows_x * rows_y, depth), z_forward, y_forward)
-
     weights = spectral_weight.reshape(pair_rows * MX, -1)
     weights = jnp.pad(weights, [(0, wide - pair_rows * MX), (0, 0)])
+    state = plume_state.reshape(fields, cells_xy, depth)
     sems = pltpu.SemaphoreType.DMA((count,))
-    cells = pl.pallas_call(
-        functools.partial(modes_kernel, n_gx, n_gy, snapshots, channels),
-        out_shape=jax.ShapeDtypeStruct((fields * MZ, blocks * LANES), BF16),
-        in_specs=[whole] * 4,
-        out_specs=whole,
+    cells, local = pl.pallas_call(
+        functools.partial(modes_kernel, n_gx, n_gy, snapshots, channels, group),
+        out_shape=(
+            jax.ShapeDtypeStruct((fields * MZ, blocks * LANES), BF16),
+            jax.ShapeDtypeStruct(state.shape, F32),
+        ),
+        in_specs=[anywhere, whole, whole, anywhere, anywhere, anywhere, whole, whole],
+        out_specs=(whole, anywhere),
         scratch_shapes=[
+            pltpu.VMEM(state.shape, BF16),
+            pltpu.VMEM(weights.shape, BF16),
+            pltpu.VMEM(x_forward.shape, BF16),
+            pltpu.VMEM(x_back.shape, BF16),
+            pltpu.VMEM((blocks, slot * MZ, LANES), F32),
+            pltpu.VMEM((count, slot, LANES), BF16),
             pltpu.VMEM((count, slot, LANES), BF16),
             pltpu.VMEM((count, slot, LANES), BF16),
             pltpu.VMEM((n_gx, slot, LANES), BF16),
@@ -324,30 +360,35 @@
             pltpu.VMEM((slot, 2 * wide), F32),
             pltpu.VMEM((slot, 2 * wide), F32),
             pltpu.VMEM((blocks, fields * MZ, LANES), F32),
+            pltpu.VMEM(state.shape, F32),
+            pltpu.VMEM((channels * TILE, channels * TILE), BF16),
+            pltpu.SemaphoreType.DMA((steps,)),
+            pltpu.SemaphoreType.DMA((3,)),
+            pltpu.SemaphoreType.DMA((snapshots,)),
             sems, sems, sems, sems,
         ],
         compiler_params=pltpu.CompilerParams(
             vmem_limit_bytes=limit, collective_id=0, has_side_effects=True
         ),
         name="modes",
-    )(sent, weights, x_forward, x_back)
-
-    pointwise = (
-        pointwise_weight.T[:, None, :, None] * jnp.eye(TILE, dtype=BF16)[None, :, None, :]
-    ).reshape(channels * TILE, channels * TILE)
-    bias = jnp.broadcast_to(channel_bias[:, None, None], (channels, 1, depth))
-    state = plume_state.reshape(fields, rows_x, rows_y, depth)
-    slab = pl.BlockSpec((fields, 1, rows_y, depth), lambda x: (0, x, 0, 0))
+    )(state, z_forward, y_forward, weights, x_forward, x_back, pointwise_weight, spread)
+
+    slab = pl.BlockSpec((group, cells_xy, depth), lambda g: (g, 0, 0))
     result = pl.pallas_call(
-        functools.partial(inverse_kernel, snapshots, channels),
-        grid=(rows_x,),
+        functools.partial(inverse_kernel, channels),
+        grid=(steps,),
         out_shape=jax.ShapeDtypeStruct(state.shape, BF16),
-        in_specs=[slab] + [whole] * 5,
+        in_specs=[
+            slab,
+            pl.BlockSpec((group * MZ, blocks * LANES), lambda g: (g, 0)),
+            whole,
+            whole,
+            pl.BlockSpec(memory_space=pltpu.SMEM),
+        ],
         out_specs=slab,
-        scratch_shapes=[pltpu.VMEM((fields, rows_y, depth), F32)],
         compiler_params=pltpu.CompilerParams(vmem_limit_bytes=limit),
         name="inverse",
-    )(state, cells, y_back, z_back, pointwise, bias)
+    )(local, cells, y_back, z_back, channel_bias)
     return result.reshape(plume_state.shape)
 
 

time: 46 us -> 36.5 us (0.79)
  Pallas kernels: 40.8 us -> 36.2 us
  local copies, waits for them, and re-layouts: 4.47 us -> 0 us
    pallas_call x2 -> x1, Pallas kernels: 19.6 us -> 12.4 us  [body(): pl.pallas_call(functools.partial(inverse_kernel, channels), grid=(steps,)...]
    pallas_call x1, Pallas kernels: 21.2 us -> 23.8 us  [body(): pl.pallas_call(functools.partial(modes_kernel, n_gx, n_gy, snapshots, cha...]
    unnamed x12 -> x0, local copies, waits for them, and re-layouts: 1.76 us -> none
    mul x1 -> x0, local copies, waits for them, and re-layouts: 1.2 us -> none  [body(): pointwise_weight.T[:, None, :, None]]
    transpose x1 -> x0, local copies, waits for them, and re-layouts: 0.79 us -> none  [body(): pointwise_weight.T[:, None, :, None]]
    broadcast_in_dim x1 -> x0, local copies, waits for them, and re-layouts: 0.73 us -> none  [body(): bias = jnp.broadcast_to(channel_bias[:, None, None], (channels, 1, depth))]
where the time goes in v2:
time: 36.5 us; the launch traced here: 36.2 us
  Pallas kernels  36.2 us (99%)
    pallas_call x1, Pallas kernels, body(): pl.pallas_call(functools.partial(modes_kernel, n_gx, n_gy, snapshots, cha...  23.8 us
    pallas_call x1, Pallas kernels, body(): pl.pallas_call(functools.partial(inverse_kernel, channels), grid=(steps,)...  12.4 us

profile of v2, /device:TPU:0, one launch (start us, length us, event | category | flops | bytes accessed | tf_op | source)
XLA Modules:
  0.0 36.2 jit_solution(15748691422786506926)
XLA Ops:
  0.0 23.8 %modes.1 = (bf16[640,128]{1,0:T(8,128)(2,1)}, f32[40,512,128]{2,1,0:T(8,128)}) custom-call(bf16[40,512,128]{2,1,0:T(8,128)(2,1)} %bitcast.3, bf16[32,128]{1,0:T(8,128)(2,1)} %constant.7.clone.z_forward, bf16[2,1024,128]{2,1,0:T(8,128)(2,1)} %constant.16.clone.y_forward, bf16[384,800]{1,0:T(8,128)(2,1)} %bitcast.4, ...), custom_call_target="tpu_custom_call" | custom-call | tf_op jit(solution)/shard_map/modes/pallas_call | solution.py:341
  23.8 12.4 %inverse.1 = bf16[40,512,128]{2,1,0:T(8,128)(2,1)} custom-call(f32[40,512,128]{2,1,0:T(8,128)} %get-tuple-element.7.local, bf16[640,128]{1,0:T(8,128)(2,1)} %get-tuple-element.8.cells, bf16[2,2,512,128]{3,2,1,0:T(8,128)(2,1)} %constant.19.clone.y_back, bf16[256,1024]{1,0:T(8,128)(2,1)} %constant.20.clone.z_back, f32[20]{0:T(128)} %bias.1), custom_call_target="tpu_custom_call" | custom-call | tf_op jit(solution)/shard_map/inverse/pallas_call | solution.py:377

commit v3 on v2

--- a/solution.py
+++ b/solution.py
@@ -15,6 +15,7 @@
 MZ = 16
 LANES = 128
 TILE = 16
+HALF = 8
 MESH = pl.DeviceIdType.MESH
 F32 = jnp.float32
 BF16 = jnp.bfloat16
@@ -152,10 +153,10 @@
         pl.semaphore_signal(barrier, inc=1, device_id=device(peer), device_id_type=MESH)
 
     each(count, greet)
-    size = channels * TILE
+    size = channels * HALF
     scaled = dot_lanes(dot_lanes(spread[...], pointwise[...]).astype(BF16), spread[...])
-    at_row = lax.broadcasted_iota(jnp.int32, (size, size), 0) % TILE
-    at_column = lax.broadcasted_iota(jnp.int32, (size, size), 1) % TILE
+    at_row = lax.broadcasted_iota(jnp.int32, (size, size), 0) % HALF
+    at_column = lax.broadcasted_iota(jnp.int32, (size, size), 1) % HALF
     kron[...] = jnp.where(at_row == at_column, scaled, 0.0).astype(BF16)
 
     rows[:, pl.ds(fields * MZ, (slot_rows - fields) * MZ), :] = jnp.zeros(
@@ -185,23 +186,22 @@
         fld = pl.ds(t * channels, channels)
 
         def strip(i, _):
-            base = pl.multiple_of(i * 2 * TILE, 2 * TILE)
-            block = plume[fld, pl.ds(base, 2 * TILE), :]
+            base = pl.ds(pl.multiple_of(i * TILE, TILE), TILE)
+            block = plume[fld, base, :].astype(F32)
             pair = jnp.concatenate(
+                [block[:, h : h + HALF].reshape(size, depth) for h in (0, HALF)], axis=1
+            )
+            value = dot(kron[...], pair.astype(BF16))
+            local[fld, base, :] = jnp.concatenate(
                 [
-                    block[:, :TILE].reshape(size, depth),
-                    block[:, TILE:].reshape(size, depth),
+                    value[:, h : h + depth].reshape(channels, HALF, depth)
+                    for h in (0, depth)
                 ],
                 axis=1,
-            )
-            value = dot(kron[...], pair)
-            for h in range(2):
-                local[fld, pl.ds(base + h * TILE, TILE), :] = value[
-                    :, h * depth : (h + 1) * depth
-                ].reshape(channels, TILE, depth)
+            ).astype(BF16)
             return 0
 
-        lax.fori_loop(0, plume.shape[1] // (2 * TILE), strip, 0)
+        lax.fori_loop(0, plume.shape[1] // TILE, strip, 0, unroll=8)
         local_copy(t).start()
 
     def local_copy(t):
@@ -286,19 +286,9 @@
         local_copy(t).wait()
 
 
-E = (
-    0.797884268412902, 0.03633414910206053, -3.3026689185494805e-05, -5.527339041578515e-05,
-    3.974071266817981e-06, -1.3378326030725087e-07, 1.8139279592266355e-09,
-)
-
-
 def gelu(x):
-    square = jnp.minimum(x * x, 30.25)
-    series = jnp.full_like(x, E[-1])
-    for term in E[-2::-1]:
-        series = series * square + term
     half = 0.5 * x
-    return half + half * jnp.tanh(x * series)
+    return half + half * lax.erf(x * math.sqrt(0.5))
 
 
 def inverse_kernel(channels, local, cells, y_back, z_back, bias, out):
@@ -312,7 +302,7 @@
         values = dot(both, z_back[:, j * depth : (j + 2) * depth])
         for h in range(2):
             level = bias[lax.rem(g * group + j + h, channels)]
-            value = values[:, h * depth : (h + 1) * depth] + local[j + h] + level
+            value = values[:, h * depth : (h + 1) * depth] + local[j + h].astype(F32) + level
             out[j + h] = gelu(value).astype(BF16)
 
 
@@ -329,7 +319,7 @@
     z_forward, y_forward, x_forward, x_back, y_back, z_back = tables(
         n_gx, n_gy, rows_x, rows_y, depth, pair_rows, group
     )
-    spread = jnp.asarray(np.repeat(np.eye(channels), TILE, axis=0).astype(ml_dtypes.bfloat16))
+    spread = jnp.asarray(np.repeat(np.eye(channels), HALF, axis=0).astype(ml_dtypes.bfloat16))
     whole = pl.BlockSpec(memory_space=pltpu.VMEM)
     anywhere = pl.BlockSpec(memory_space=pl.ANY)
     limit = 60 * 2**20
@@ -342,7 +332,7 @@
         functools.partial(modes_kernel, n_gx, n_gy, snapshots, channels, group),
         out_shape=(
             jax.ShapeDtypeStruct((fields * MZ, blocks * LANES), BF16),
-            jax.ShapeDtypeStruct(state.shape, F32),
+            jax.ShapeDtypeStruct(state.shape, BF16),
         ),
         in_specs=[anywhere, whole, whole, anywhere, anywhere, anywhere, whole, whole],
         out_specs=(whole, anywhere),
@@ -360,8 +350,8 @@
             pltpu.VMEM((slot, 2 * wide), F32),
             pltpu.VMEM((slot, 2 * wide), F32),
             pltpu.VMEM((blocks, fields * MZ, LANES), F32),
-            pltpu.VMEM(state.shape, F32),
-            pltpu.VMEM((channels * TILE, channels * TILE), BF16),
+            pltpu.VMEM(state.shape, BF16),
+            pltpu.VMEM((channels * HALF, channels * HALF), BF16),
             pltpu.SemaphoreType.DMA((steps,)),
             pltpu.SemaphoreType.DMA((3,)),
             pltpu.SemaphoreType.DMA((snapshots,)),

time: 36.5 us -> 32 us (0.88)
  Pallas kernels: 36.2 us -> 31.8 us
    pallas_call x1, Pallas kernels: 12.4 us -> 8.53 us  [body(): pl.pallas_call(functools.partial(inverse_kernel, channels), grid=(steps,)...]
    pallas_call x1, Pallas kernels: 23.8 us -> 23.2 us  [body(): pl.pallas_call(functools.partial(modes_kernel, n_gx, n_gy, snapshots, cha...]
where the time goes in v3:
time: 32 us; the launch traced here: 31.8 us
  Pallas kernels  31.8 us (99%)
    pallas_call x1, Pallas kernels, body(): pl.pallas_call(functools.partial(modes_kernel, n_gx, n_gy, snapshots, cha...  23.2 us
    pallas_call x1, Pallas kernels, body(): pl.pallas_call(functools.partial(inverse_kernel, channels), grid=(steps,)...  8.53 us

profile of v3, /device:TPU:0, one launch (start us, length us, event | category | flops | bytes accessed | tf_op | source)
XLA Modules:
  0.0 31.8 jit_solution(5721322583394610235)
XLA Ops:
  0.0 23.2 %modes.1 = (bf16[640,128]{1,0:T(8,128)(2,1)}, bf16[40,512,128]{2,1,0:T(8,128)(2,1)}) custom-call(bf16[40,512,128]{2,1,0:T(8,128)(2,1)} %bitcast.3, bf16[32,128]{1,0:T(8,128)(2,1)} %constant.7.clone.z_forward, bf16[2,1024,128]{2,1,0:T(8,128)(2,1)} %constant.16.clone.y_forward, bf16[384,800]{1,0:T(8,128)(2,1)} %bitcast.4, ...), custom_call_target="tpu_custom_call" | custom-call | tf_op jit(solution)/shard_map/modes/pallas_call | solution.py:331
  23.3 8.5 %inverse.1 = bf16[40,512,128]{2,1,0:T(8,128)(2,1)} custom-call(bf16[40,512,128]{2,1,0:T(8,128)(2,1)} %get-tuple-element.7.local, bf16[640,128]{1,0:T(8,128)(2,1)} %get-tuple-element.8.cells, bf16[2,2,512,128]{3,2,1,0:T(8,128)(2,1)} %constant.19.clone.y_back, bf16[256,1024]{1,0:T(8,128)(2,1)} %constant.20.clone.z_back, f32[20]{0:T(128)} %bias.1), custom_call_target="tpu_custom_call" | custom-call | tf_op jit(solution)/shard_map/inverse/pallas_call | solution.py:367

commit v4 on v3

--- a/solution.py
+++ b/solution.py
@@ -117,7 +117,7 @@
     out, local_out,
     plume, weights, x_forward, x_back, rows, sent,
     landed, back, going, mixers, pairs, mixed, order, local, kron,
-    in_sem, table_sem, local_sem, send_one, recv_one, send_two, recv_two,
+    in_sem, table_sem, local_sem, send_one, recv_one, send_two, recv_two, send_on, recv_on,
 ):
     count = n_gx * n_gy
     my_x, my_y = lax.axis_index("gx"), lax.axis_index("gy")
@@ -127,6 +127,7 @@
     blocks = count // MZ
     slot_rows = sent.shape[1]
     steps = fields // group
+    parts_out = slot_rows // TILE
 
     def device(index):
         return {"gx": lax.rem(index, n_gx), "gy": lax.div(index, n_gx)}
@@ -158,6 +159,49 @@
     at_row = lax.broadcasted_iota(jnp.int32, (size, size), 0) % HALF
     at_column = lax.broadcasted_iota(jnp.int32, (size, size), 1) % HALF
     kron[...] = jnp.where(at_row == at_column, scaled, 0.0).astype(BF16)
+
+    def first(s, at, part):
+        peer = lax.rem(me + s, count)
+        band = pl.ds(part * TILE, TILE)
+        return pltpu.make_async_remote_copy(
+            src_ref=sent.at[peer, band], dst_ref=landed.at[at, band],
+            send_sem=send_one.at[part, s], recv_sem=recv_one.at[part, s],
+            device_id=device(peer), device_id_type=MESH,
+        )
+
+    def send_part(part):
+        band = pl.ds(part * TILE, TILE)
+        for kz in range(MZ):
+            for block in range(blocks):
+                taken = rows[block, pl.ds(part * TILE * MZ + kz, TILE, stride=MZ), :]
+                sent[kz * blocks + block, band, :] = taken.astype(BF16)
+        if part == 0:
+            pl.semaphore_wait(barrier, count - 1)
+        each(count, lambda s: first(s, me, part).start())
+
+    def second(s, at):
+        peer = lax.rem(my_x + s, n_gx)
+        return pltpu.make_async_remote_copy(
+            src_ref=going.at[peer], dst_ref=back.at[at],
+            send_sem=send_two.at[s], recv_sem=recv_two.at[s],
+            device_id={"gx": peer}, device_id_type=MESH,
+        )
+
+    def onward(h, s, owner_y):
+        at = owner_y * n_gx + lax.rem(my_x + n_gx - s, n_gx)
+        return pltpu.make_async_remote_copy(
+            src_ref=back.at[at], dst_ref=back.at[at],
+            send_sem=send_on.at[h, s], recv_sem=recv_on.at[h, s],
+            device_id={"gy": lax.rem(my_y + h, n_gy)}, device_id_type=MESH,
+        )
+
+    def arrived(s):
+        second(s, my_y * n_gx + lax.rem(my_x + n_gx - s, n_gx)).wait_recv()
+        for h in range(1, n_gy):
+            onward(h, s, my_y).start()
+
+    def source(s):
+        return lax.rem(me + count - s, count)
 
     rows[:, pl.ds(fields * MZ, (slot_rows - fields) * MZ), :] = jnp.zeros(
         (blocks, (slot_rows - fields) * MZ, LANES), F32
@@ -173,12 +217,10 @@
             rows[block, pl.ds(g * group * MZ, group * MZ), :] = terms[
                 :, block * LANES : (block + 1) * LANES
             ]
-    for kz in range(MZ):
-        for block in range(blocks):
-            sent[kz * blocks + block] = rows[block, pl.ds(kz, slot_rows, stride=MZ), :].astype(
-                BF16
-            )
-    pl.semaphore_wait(barrier, count - 1)
+        for part in range(parts_out):
+            ready = min(-(-(part + 1) * TILE // group), steps) - 1
+            if ready == g:
+                send_part(part)
 
     depth = plume.shape[2]
 
@@ -208,26 +250,6 @@
         fld = pl.ds(t * channels, channels)
         return pltpu.make_async_copy(local.at[fld], local_out.at[fld], local_sem.at[t])
 
-    def first(s, at):
-        peer = lax.rem(me + s, count)
-        return pltpu.make_async_remote_copy(
-            src_ref=sent.at[peer], dst_ref=landed.at[at],
-            send_sem=send_one.at[s], recv_sem=recv_one.at[s],
-            device_id=device(peer), device_id_type=MESH,
-        )
-
-    def second(s, at):
-        peer = lax.rem(me + s, count)
-        return pltpu.make_async_remote_copy(
-            src_ref=going.at[lax.rem(peer, n_gx)], dst_ref=back.at[at],
-            send_sem=send_two.at[s], recv_sem=recv_two.at[s],
-            device_id=device(peer), device_id_type=MESH,
-        )
-
-    def source(s):
-        return lax.rem(me + count - s, count)
-
-    each(count, lambda s: first(s, me).start())
     landed[me] = sent[me]
 
     for copy in held:
@@ -241,7 +263,8 @@
         mixers[pl.ds(at, LANES), :] = chunk.T
     pointwise_of(0)
 
-    each(count, lambda s: first(s, source(s)).wait_recv())
+    for part in range(parts_out):
+        each(count, lambda s, part=part: first(s, source(s), part).wait_recv())
     summed = []
     for i in range(n_gx):
         total = landed[i].astype(F32)
@@ -268,11 +291,17 @@
     for i in range(n_gx):
         going[i] = cells[:, i * LANES : (i + 1) * LANES]
 
-    each(count, lambda s: second(s, me).start())
+    each(n_gx, lambda s: second(s, me).start())
     back[me] = going[my_x]
+    for h in range(1, n_gy):
+        onward(h, 0, my_y).start()
     for t in range(1, snapshots):
         pointwise_of(t)
-    each(count, lambda s: second(s, source(s)).wait_recv())
+    each(n_gx, arrived)
+    for h in range(1, n_gy):
+        owner_y = lax.rem(my_y + n_gy - h, n_gy)
+        onward(h, 0, owner_y).wait_recv()
+        each(n_gx, lambda s, h=h, owner_y=owner_y: onward(h, s, owner_y).wait_recv())
     for kz in range(MZ):
         for block in range(blocks):
             order[block, pl.ds(kz, fields, stride=MZ), :] = back[kz * blocks + block].astype(
@@ -280,8 +309,12 @@
             )[:fields]
     for block in range(blocks):
         out[:, pl.ds(block * LANES, LANES)] = order[block].astype(BF16)
-    each(count, lambda s: first(s, me).wait_send())
-    each(count, lambda s: second(s, me).wait_send())
+    for part in range(parts_out):
+        each(count, lambda s, part=part: first(s, me, part).wait_send())
+    each(n_gx, lambda s: second(s, me).wait_send())
+    for h in range(1, n_gy):
+        onward(h, 0, my_y).wait_send()
+        each(n_gx, lambda s, h=h: onward(h, s, my_y).wait_send())
     for t in range(snapshots):
         local_copy(t).wait()
 
@@ -327,7 +360,9 @@
     weights = spectral_weight.reshape(pair_rows * MX, -1)
     weights = jnp.pad(weights, [(0, wide - pair_rows * MX), (0, 0)])
     state = plume_state.reshape(fields, cells_xy, depth)
-    sems = pltpu.SemaphoreType.DMA((count,))
+    many = pltpu.SemaphoreType.DMA((slot // TILE, count))
+    few = pltpu.SemaphoreType.DMA((n_gx,))
+    chain = pltpu.SemaphoreType.DMA((n_gy, n_gx))
     cells, local = pl.pallas_call(
         functools.partial(modes_kernel, n_gx, n_gy, snapshots, channels, group),
         out_shape=(
@@ -355,7 +390,7 @@
             pltpu.SemaphoreType.DMA((steps,)),
             pltpu.SemaphoreType.DMA((3,)),
             pltpu.SemaphoreType.DMA((snapshots,)),
-            sems, sems, sems, sems,
+            many, many, few, few, chain, chain,
         ],
         compiler_params=pltpu.CompilerParams(
             vmem_limit_bytes=limit, collective_id=0, has_side_effects=True

time: 32 us -> 31.2 us (0.975)
  Pallas kernels: 31.8 us -> 30.8 us
    pallas_call x1, Pallas kernels: 23.2 us -> 22.3 us  [body(): pl.pallas_call(functools.partial(modes_kernel, n_gx, n_gy, snapshots, cha...]
where the time goes in v4:
time: 31.2 us; the launch traced here: 30.8 us
  Pallas kernels  30.8 us (99%)
    pallas_call x1, Pallas kernels, body(): pl.pallas_call(functools.partial(modes_kernel, n_gx, n_gy, snapshots, cha...  22.3 us
    pallas_call x1, Pallas kernels, body(): pl.pallas_call(functools.partial(inverse_kernel, channels), grid=(steps,)...  8.52 us

profile of v4, /device:TPU:0, one launch (start us, length us, event | category | flops | bytes accessed | tf_op | source)
XLA Modules:
  0.0 30.8 jit_solution(2157139808334701244)
XLA Ops:
  0.0 22.3 %modes.1 = (bf16[640,128]{1,0:T(8,128)(2,1)}, bf16[40,512,128]{2,1,0:T(8,128)(2,1)}) custom-call(bf16[40,512,128]{2,1,0:T(8,128)(2,1)} %bitcast.3, bf16[32,128]{1,0:T(8,128)(2,1)} %constant.7.clone.z_forward, bf16[2,1024,128]{2,1,0:T(8,128)(2,1)} %constant.16.clone.y_forward, bf16[384,800]{1,0:T(8,128)(2,1)} %bitcast.4, ...), custom_call_target="tpu_custom_call" | custom-call | tf_op jit(solution)/shard_map/modes/pallas_call | solution.py:366
  22.3 8.5 %inverse.1 = bf16[40,512,128]{2,1,0:T(8,128)(2,1)} custom-call(bf16[40,512,128]{2,1,0:T(8,128)(2,1)} %get-tuple-element.7.local, bf16[640,128]{1,0:T(8,128)(2,1)} %get-tuple-element.8.cells, bf16[2,2,512,128]{3,2,1,0:T(8,128)(2,1)} %constant.19.clone.y_back, bf16[256,1024]{1,0:T(8,128)(2,1)} %constant.20.clone.z_back, f32[20]{0:T(128)} %bias.1), custom_call_target="tpu_custom_call" | custom-call | tf_op jit(solution)/shard_map/inverse/pallas_call | solution.py:402

commit v5 on v4

--- a/solution.py
+++ b/solution.py
@@ -127,7 +127,8 @@
     blocks = count // MZ
     slot_rows = sent.shape[1]
     steps = fields // group
-    parts_out = slot_rows // TILE
+    bands = [(at, min(2 * TILE, slot_rows - at)) for at in range(0, slot_rows, 2 * TILE)]
+    parts_out = len(bands)
 
     def device(index):
         return {"gx": lax.rem(index, n_gx), "gy": lax.div(index, n_gx)}
@@ -162,7 +163,7 @@
 
     def first(s, at, part):
         peer = lax.rem(me + s, count)
-        band = pl.ds(part * TILE, TILE)
+        band = pl.ds(*bands[part])
         return pltpu.make_async_remote_copy(
             src_ref=sent.at[peer, band], dst_ref=landed.at[at, band],
             send_sem=send_one.at[part, s], recv_sem=recv_one.at[part, s],
@@ -170,10 +171,11 @@
         )
 
     def send_part(part):
-        band = pl.ds(part * TILE, TILE)
+        band = pl.ds(*bands[part])
         for kz in range(MZ):
             for block in range(blocks):
-                taken = rows[block, pl.ds(part * TILE * MZ + kz, TILE, stride=MZ), :]
+                at, size = bands[part]
+                taken = rows[block, pl.ds(at * MZ + kz, size, stride=MZ), :]
                 sent[kz * blocks + block, band, :] = taken.astype(BF16)
         if part == 0:
             pl.semaphore_wait(barrier, count - 1)
@@ -218,13 +220,13 @@
                 :, block * LANES : (block + 1) * LANES
             ]
         for part in range(parts_out):
-            ready = min(-(-(part + 1) * TILE // group), steps) - 1
+            ready = min(-(-sum(bands[part]) // group), steps) - 1
             if ready == g:
                 send_part(part)
 
     depth = plume.shape[2]
 
-    def pointwise_of(t):
+    def pointwise_of(t, piece=0, pieces=1):
         fld = pl.ds(t * channels, channels)
 
         def strip(i, _):
@@ -243,8 +245,10 @@
             ).astype(BF16)
             return 0
 
-        lax.fori_loop(0, plume.shape[1] // TILE, strip, 0, unroll=8)
-        local_copy(t).start()
+        strips = plume.shape[1] // TILE // pieces
+        lax.fori_loop(piece * strips, (piece + 1) * strips, strip, 0, unroll=8)
+        if piece == pieces - 1:
+            local_copy(t).start()
 
     def local_copy(t):
         fld = pl.ds(t * channels, channels)
@@ -296,8 +300,10 @@
     for h in range(1, n_gy):
         onward(h, 0, my_y).start()
     for t in range(1, snapshots):
-        pointwise_of(t)
+        pointwise_of(t, 0, 2)
     each(n_gx, arrived)
+    for t in range(1, snapshots):
+        pointwise_of(t, 1, 2)
     for h in range(1, n_gy):
         owner_y = lax.rem(my_y + n_gy - h, n_gy)
         onward(h, 0, owner_y).wait_recv()

time: 31.2 us -> 32 us (1.026)
  Pallas kernels: 30.8 us -> 31.8 us
    pallas_call x1, Pallas kernels: 22.3 us -> 23.3 us  [body(): pl.pallas_call(functools.partial(modes_kernel, n_gx, n_gy, snapshots, cha...]
where the time goes in v5:
time: 32 us; the launch traced here: 31.8 us
  Pallas kernels  31.8 us (99%)
    pallas_call x1, Pallas kernels, body(): pl.pallas_call(functools.partial(modes_kernel, n_gx, n_gy, snapshots, cha...  23.3 us
    pallas_call x1, Pallas kernels, body(): pl.pallas_call(functools.partial(inverse_kernel, channels), grid=(steps,)...  8.53 us

profile of v5, /device:TPU:0, one launch (start us, length us, event | category | flops | bytes accessed | tf_op | source)
XLA Modules:
  0.0 31.8 jit_solution(12842383940493243294)
XLA Ops:
  0.0 23.3 %modes.1 = (bf16[640,128]{1,0:T(8,128)(2,1)}, bf16[40,512,128]{2,1,0:T(8,128)(2,1)}) custom-call(bf16[40,512,128]{2,1,0:T(8,128)(2,1)} %bitcast.3, bf16[32,128]{1,0:T(8,128)(2,1)} %constant.7.clone.z_forward, bf16[2,1024,128]{2,1,0:T(8,128)(2,1)} %constant.16.clone.y_forward, bf16[384,800]{1,0:T(8,128)(2,1)} %bitcast.4, ...), custom_call_target="tpu_custom_call" | custom-call | tf_op jit(solution)/shard_map/modes/pallas_call | solution.py:372
  23.3 8.5 %inverse.1 = bf16[40,512,128]{2,1,0:T(8,128)(2,1)} custom-call(bf16[40,512,128]{2,1,0:T(8,128)(2,1)} %get-tuple-element.7.local, bf16[640,128]{1,0:T(8,128)(2,1)} %get-tuple-element.8.cells, bf16[2,2,512,128]{3,2,1,0:T(8,128)(2,1)} %constant.19.clone.y_back, bf16[256,1024]{1,0:T(8,128)(2,1)} %constant.20.clone.z_back, f32[20]{0:T(128)} %bias.1), custom_call_target="tpu_custom_call" | custom-call | tf_op jit(solution)/shard_map/inverse/pallas_call | solution.py:408
